TPU v7x, 512 devices: a whole 4x4x16 slice. The times are simulated.
512 devices in a mesh: row: 8 (over y, core), col: 32 (over z_lo, x), leaf: 2 (over z_hi).
Axes of the slice: x: 4, y: 4, z: 16 (z_hi: 2, z_lo: 8; z = z_hi * 8 + z_lo), core: 2. Of those that a mesh axis runs over, the one named last changes fastest.
Arguments:
- ancestor: bfloat16 [8192, 8192], P('row', ('col', 'leaf')), may hold values from -2 to 42, as said below
- factor: bfloat16 [8, 8192, 512], P(None, ('row', 'col', 'leaf')), may hold values from -0.03125 to 0.03125
- inv_diag: bfloat16 [8, 512, 512], replicated, may hold values from -0.4 to 2, as said below
- pattern: int32 [8, 32], replicated, may hold values 0 or 1
Outputs:
- sigma_panel: float32 [8, 8192, 512], P('row', ('col', 'leaf'))
- sigma_diag: float32 [8, 512, 512], P('row', ('col', 'leaf'))
Inputs may be any that keep to these rules, and one draw needn't show every extreme that they name: ancestor is symmetric. Each inv_diag[j] is lower triangular with a positive diagonal.
All inputs are finite; a program needn't handle non-finite values.
Results may differ from a plain program's by a relative error of at most 0.0029.
Values may be sent and summed in bfloat16 or wider, within the bound.
A program may use at most 64 MiB of HBM per device.

v0:
```python
import jax
import jax.numpy as jnp
from jax import lax
from jax.sharding import PartitionSpec as P

BLOCK = 256


def spread(x, axis, root):
    mine = lax.axis_index(axis) == root
    return lax.psum(jnp.where(mine, x, jnp.zeros_like(x)), axis)


def block_flags(pattern, first_row, row_total, block_size):
    blocks = (first_row + jnp.arange(row_total, dtype=jnp.int32)) // block_size
    matches = blocks[:, None] == jnp.arange(pattern.shape[1], dtype=jnp.int32)[None, :]
    return jnp.sum(jnp.where(matches[None, :, :], pattern[:, None, :], 0), axis=2) > 0


def ship_rows(gathered, col_index, row_index, group_span, band_cols):
    leader = col_index // group_span
    offset = col_index % group_span * band_cols
    section = lax.dynamic_slice_in_dim(gathered, offset, band_cols, 1)
    shipped = spread(section, "row", leader)
    return lax.dynamic_slice_in_dim(shipped, row_index, 1, 0)[0]


def body(ancestor, factor, inv_diag, pattern):
    row_count = lax.axis_size("row")
    col_count = lax.axis_size(("col", "leaf"))
    row_index = lax.axis_index("row")
    col_index = lax.axis_index(("col", "leaf"))
    children, local_rows, columns = factor.shape
    band_rows, band_cols = ancestor.shape
    group_span = col_count // row_count
    first_row = row_index * band_rows + col_index * local_rows
    kept_rows = block_flags(pattern, first_row, local_rows, BLOCK)
    masked = jnp.where(kept_rows[:, :, None], factor, jnp.zeros_like(factor))
    local_panel = jnp.einsum(
        "jsk,jkn->jsn", masked, inv_diag, preferred_element_type=jnp.float32
    ).astype(jnp.bfloat16)
    gathered = lax.all_gather(local_panel, ("col", "leaf"), axis=1, tiled=True)
    products = jnp.einsum("sc,jsk->jck", ancestor, gathered, preferred_element_type=jnp.float32)
    summed = lax.psum_scatter(products, "row", scatter_dimension=0, tiled=True)
    own_panel = ship_rows(gathered, col_index, row_index, group_span, band_cols)
    panel_flags = block_flags(pattern, col_index * band_cols, band_cols, BLOCK)
    own_flags = lax.dynamic_slice_in_dim(panel_flags, row_index, 1, 0)
    sigma_panel = -jnp.where(own_flags[:, :, None], summed, jnp.zeros_like(summed))
    rounded = summed[0].astype(jnp.bfloat16)
    contract = (((0,), (0,)), ((), ()))
    cross = lax.dot_general(own_panel, rounded, contract, preferred_element_type=jnp.float32)
    own_inverse = lax.dynamic_slice_in_dim(inv_diag, row_index, 1, 0)[0]
    share = columns // col_count
    inverse_rows = lax.dynamic_slice_in_dim(own_inverse, col_index * share, share, 0)
    square = lax.dot_general(
        inverse_rows, inverse_rows, contract, preferred_element_type=jnp.float32
    )
    summand = cross + square
    diag_part = lax.psum_scatter(summand, ("col", "leaf"), scatter_dimension=0, tiled=True)
    sigma_diag = diag_part[None]
    return (sigma_panel, sigma_diag)


def solution(mesh):
    return jax.shard_map(
        body,
        mesh=mesh,
        in_specs=(P("row", ("col", "leaf")), P(None, ("row", "col", "leaf"), None), P(), P()),
        out_specs=(P("row", ("col", "leaf"), None), P("row", ("col", "leaf"), None)),
        check_vma=False,
    )
```

profile of v0, /device:TPU:24, one launch (start us, length us, event | category | flops | bytes accessed | tf_op | source)
XLA Modules:
  0.0 1719.5 jit_solution(2166982286237987865)
XLA Ops:
  7.2 0.0 copy-start
  7.2 0.0 all-gather.2.cloned.1.call-start
  7.3 0.1 iota_compare_fusion.1
  7.3 0.9 select_reduce_fusion.1
  8.2 3.6 convolution_convert_fusion
  11.9 0.0 all-gather.2.cloned.1.call-update
  11.9 0.0 all-reduce.2.cloned.1.call-start
  12.0 1060.3 %all-gather.2.cloned.1.call-done = bf16[8,1024,512]{2,1,0:T(8,128)(2,1)} async-done(((bf16[8,16,512]{2,1,0:T(8,128)(2,1)}), bf16[8,1024,512]{2,1,0:T(8,128)(2,1)}) %all-gather.2.cloned.1.call-update) | async-done | bytes 8388624 | tf_op jit(solution)/shard_map/all_gather | solution.py:42
  1072.3 2.4 dynamic-slice_select_fusion
  1074.7 0.0 all-reduce.2.cloned.1.call-update
  1074.7 0.0 reduce-scatter.3.cloned.1.call-start
  1074.8 0.0 copy-done
  1074.8 7.2 convolution_bitcast_fusion
  1081.9 0.0 copy-start.2
  1081.9 0.0 reduce-scatter.3.cloned.1.call-update
  1082.0 0.0 reduce-scatter.5.cloned.1.call-start
  1082.0 79.9 %all-reduce.2.cloned.1.call-done = bf16[8,128,512]{2,1,0:T(8,128)(2,1)} async-done(((bf16[8,128,512]{2,1,0:T(8,128)(2,1)}), bf16[8,128,512]{2,1,0:T(8,128)(2,1)}) %all-reduce.2.cloned.1.call-update) | async-done | bytes 1048592 | tf_op jit(solution)/shard_map/psum | solution.py:11
  1161.9 42.6 %reduce-scatter.3.cloned.1.call-done = f32[1,128,512]{1,2,0:T(8,128)} async-done(((f32[8,128,512]{1,2,0:T(8,128)}), f32[1,128,512]{1,2,0:T(8,128)}) %reduce-scatter.3.cloned.1.call-update) | async-done | bytes 262160 | tf_op jit(solution)/shard_map/reduce_scatter | solution.py:44
  1204.5 0.0 copy-start.1
  1204.5 1.4 fusion.1
  1205.8 2.1 convolution_add_fusion
  1208.0 0.0 reduce-scatter.5.cloned.1.call-update
  1208.0 0.0 copy-done.2
  1208.0 0.1 select_reduce_fusion
  1208.2 0.0 copy-done.1
  1208.2 0.8 copy.7
  1209.1 503.9 %reduce-scatter.5.cloned.1.call-done = f32[8,512]{1,0:T(8,128)} async-done(((f32[512,512]{1,0:T(8,128)}), f32[8,512]{1,0:T(8,128)}) %reduce-scatter.5.cloned.1.call-update) | async-done | bytes 16400 | tf_op jit(solution)/shard_map/reduce_scatter | solution.py:59
  (7 shorter events, 0.1 us)
Async XLA Ops:
  7.2 1067.6 %copy-start = (bf16[1024,128]{1,0:T(8,128)(2,1)S(1)}, bf16[1024,128]{1,0:T(8,128)(2,1)}, u32[]{:S(2)}) copy-start(bf16[1024,128]{1,0:T(8,128)(2,1)} %param.4) | copy-start | bytes 786436
  7.2 1065.1 %all-gather.2.cloned.1.call-start = ((), (), s32[]{:S(2)}) async-start(), calls=%async_computation.2 | async-start | bytes 8519680 | tf_op jit(solution)/shard_map/all_gather | solution.py:42
  11.9 1150.0 %all-reduce.2.cloned.1.call-start = ((), (), s32[]{:S(2)}) async-start(), calls=%async_computation.4 | async-start | bytes 2097152 | tf_op jit(solution)/shard_map/psum | solution.py:11
  1074.7 129.7 %reduce-scatter.3.cloned.1.call-start = ((), (), s32[]{:S(2)}) async-start(), calls=%async_computation.3 | async-start | bytes 2359296 | tf_op jit(solution)/shard_map/reduce_scatter | solution.py:44
  1081.9 126.1 %copy-start.2 = (s32[8,32]{1,0:T(8,128)S(1)}, s32[8,32]{1,0:T(8,128)}, u32[]{:S(2)}) copy-start(s32[8,32]{1,0:T(8,128)} %param.7) | copy-start | bytes 3076
  1082.0 631.0 %reduce-scatter.5.cloned.1.call-start = ((), (), s32[]{:S(2)}) async-start(), calls=%async_computation.5 | async-start | bytes 1064960 | tf_op jit(solution)/shard_map/reduce_scatter | solution.py:59
  1204.5 3.7 copy-start.1
Sparse Core Ops, SparseCore 0:
  12.0 1060.2 all-gather.1
  1074.8 86.9 all-reduce.1
  1164.7 39.6 reduce-scatter.2
  1208.1 504.8 reduce-scatter.4
where the time goes:
time: 1720 us
  waiting for transfers between devices  1690 us (98%)
    all_gather x1, waiting for transfers between devices, body(): gathered = lax.all_gather(local_panel, ('col', 'leaf'), axis=1, tiled=True)  1060 us
    reduce_scatter x1, waiting for transfers between devices, body(): lax.psum_scatter(summand, ('col', 'leaf'), scatter_dimension=0, tiled=True)  504 us
    psum x1, waiting for transfers between devices, spread(): return lax.psum(jnp.where(mine, x, jnp.zeros_like(x)), axis)  79.9 us
    reduce_scatter x1, waiting for transfers between devices, body(): summed = lax.psum_scatter(products, 'row', scatter_dimension=0, tiled=True)  42.6 us
  transfers between devices with their start and end apart: 4, of which 4 were waited for; matrix products, arithmetic and copies ran while one was open for 0% of the time, Pallas kernels for 0%

commit v1 on v0

v1 whole, which is shorter than its diff:
```python
import functools

import jax
import jax.numpy as jnp
from jax import lax
from jax.experimental import pallas as pl
from jax.experimental.pallas import tpu as pltpu
from jax.sharding import PartitionSpec as P

MESH = pl.DeviceIdType.MESH
NX, NY, NZ, ZLO, ZHI = 4, 4, 16, 8, 2
F32, BF16 = jnp.float32, jnp.bfloat16


def device(x, y, z, h):
    return (2 * y + h, 4 * lax.rem(z, ZLO) + x, z // ZLO)


def contract_rows(a, b):
    return lax.dot_general(a, b, (((0,), (0,)), ((), ())), preferred_element_type=F32)


def kernel(
    a_ref, factor_ref, inv_ref, pattern_ref, out_ref, diag_ref,
    at, fbuf, pn, inv_own, inv_sq, square, o_send, o_recv, pd, cross, x_send, x_recv, z_send, z_recv,
    f_ss, f_rs, a_ss, a_rs, c_ss, c_rs, r_ss, r_rs, o_ss, o_rs, p_ss, p_rs, x_ss, x_rs, z_ss, z_rs, l_sem,
):
    row, col, z_hi = lax.axis_index("row"), lax.axis_index("col"), lax.axis_index("leaf")
    y, h = row // 2, lax.rem(row, 2)
    z_lo, x = col // 4, lax.rem(col, 4)
    z = z_hi * ZLO + z_lo
    band = col * 2 + z_hi

    def send(src, dst, ss, rs, to):
        return pltpu.make_async_remote_copy(
            src_ref=src, dst_ref=dst, send_sem=ss, recv_sem=rs, device_id=to, device_id_type=MESH
        )

    inv_copy = pltpu.make_async_copy(inv_ref.at[2 * x + h], inv_own, l_sem.at[0])
    sq_copy = pltpu.make_async_copy(inv_ref.at[row], inv_sq, l_sem.at[1])
    inv_copy.start()
    sq_copy.start()

    barrier = pltpu.get_barrier_semaphore()

    def greet(to):
        pl.semaphore_signal(barrier, inc=1, device_id=to, device_id_type=MESH)

    for k in range(1, 8):
        dx, dh = k // 2, k % 2
        greet(device(lax.rem(x + dx, NX), y, z, lax.rem(h + dh, 2)))
    for k in range(1, NZ):
        greet(device(x, y, lax.rem(z + k, NZ), h))
    for k in range(1, NY):
        greet(device(y, lax.rem(y + k, NY), z, h))

    @pl.when(x != y)
    def _():
        greet(device(y, y, z, h))

    pl.semaphore_wait(barrier, 7 + 15 + 3 + jnp.where(x != y, 1, 0))

    f_copies = []
    for k in range(1, 8):
        tx, th = lax.rem(x + k // 2, NX), lax.rem(h + k % 2, 2)
        f_copies.append(
            send(factor_ref.at[2 * tx + th], fbuf.at[h, x], f_ss.at[k], f_rs.at[k], device(tx, y, z, th))
        )
        f_copies[-1].start()
    fbuf[h, x] = factor_ref[2 * x + h]

    at[h, x] = a_ref[...].T
    a_copies = []
    for k in range(1, NX):
        a_copies.append(
            send(at.at[h, x], at.at[h, x], a_ss.at[k], a_rs.at[k], device(lax.rem(x + k, NX), y, z, h))
        )
        a_copies[-1].start()
    c_copies = []

    def to_sibling(k):
        sx = lax.rem(x + NX - k, NX)
        if k:
            a_copies[k - 1].wait_recv()
        c_copies.append(send(at.at[h, sx], at.at[h, sx], c_ss.at[k], c_rs.at[k], device(x, y, z, 1 - h)))
        c_copies[-1].start()

    to_sibling(0)

    inv_copy.wait()
    for c in f_copies:
        c.wait_recv()
    child = 2 * x + h
    pieces = []
    for hh in range(2):
        keep = pattern_ref[child, 4 * (2 * y + hh) + z_lo // 2]
        rows = fbuf[hh].reshape(64, 512)
        pieces.append((rows.astype(F32) * keep.astype(F32)).astype(BF16))
    masked = jnp.concatenate(pieces, axis=0)
    panel = jnp.dot(masked, inv_own[...], preferred_element_type=F32).astype(BF16)
    panel = panel.reshape(2, 4, 16, 512)
    for hh in range(2):
        for xx in range(4):
            pn[hh, z_lo, xx, z_hi] = panel[hh, xx]

    def shard(zz, hh):
        return pn.at[hh, lax.rem(zz, ZLO), :, zz // ZLO]

    ring = {}
    last = []
    for t in range(1, 9):
        for hh in range(2):
            for d in range(2):
                if t == 8 and d != hh:
                    last.append(ring[d, t - 1, hh])
                    continue
                if t > 1:
                    ring[d, t - 1, hh].wait_recv()
                if d == 0:
                    src, to = lax.rem(z + NZ - (t - 1), NZ), lax.rem(z + 1, NZ)
                else:
                    src, to = lax.rem(z + (t - 1), NZ), lax.rem(z + NZ - 1, NZ)
                ring[d, t, hh] = send(
                    shard(src, hh), shard(src, hh), r_ss.at[d, t - 1, hh], r_rs.at[d, t - 1, hh],
                    device(x, y, to, h),
                )
                ring[d, t, hh].start()
                if t == 8:
                    last.append(ring[d, t, hh])
        if t == 1:
            sq_copy.wait()
            lanes = pl.multiple_of((band * 8) // 128 * 128, 128)
            square[...] = contract_rows(inv_sq[:, pl.ds(lanes, 128)], inv_sq[...])
        if t == 6:
            to_sibling(1)
            to_sibling(3)
        if t == 7:
            to_sibling(2)
    for c in last:
        c.wait_recv()

    holds = y == z_lo // 2
    for xx in range(NX):
        here = jnp.logical_and(xx == x, x == y)

        @pl.when(jnp.logical_and(holds, jnp.logical_not(here)))
        def _():
            send(
                pn.at[lax.rem(z_lo, 2), 2 * xx + z_hi], pd, p_ss.at[xx], p_rs.at[0], device(xx, x, z, h)
            ).start()

        @pl.when(jnp.logical_and(holds, here))
        def _():
            pd[...] = pn[lax.rem(z_lo, 2), 2 * xx + z_hi]

    for c in c_copies:
        c.wait_recv()
    for xx in range(NX):
        part = jnp.dot(at[0, xx], pn[0].reshape(1024, 512), preferred_element_type=F32)
        part += jnp.dot(at[1, xx], pn[1].reshape(1024, 512), preferred_element_type=F32)
        o_send[xx] = part.astype(BF16)
        here = jnp.logical_and(xx == x, x == y)

        @pl.when(jnp.logical_not(here))
        def _():
            send(o_send.at[xx], o_recv.at[y], o_ss.at[xx], o_rs.at[y], device(xx, x, z, h)).start()

        @pl.when(here)
        def _():
            o_recv[y] = o_send[xx]

    for yy in range(NY):

        @pl.when(jnp.logical_not(jnp.logical_and(x == y, yy == y)))
        def _():
            send(o_send.at[0], o_recv.at[yy], o_ss.at[0], o_rs.at[yy], device(x, y, z, 1 - h)).wait_recv()

    total = o_recv[0].astype(F32) + o_recv[1].astype(F32) + o_recv[2].astype(F32) + o_recv[3].astype(F32)
    keep = pattern_ref[row, col]
    out_ref[0] = total * (-keep.astype(F32))

    @pl.when(jnp.logical_not(jnp.logical_and(x == y, holds)))
    def _():
        send(pn.at[0, 0], pd, p_ss.at[0], p_rs.at[0], device(x, y, z, 1 - h)).wait_recv()

    own_panel = pd[...].reshape(128, 512)
    cross[...] = contract_rows(own_panel, total.astype(BF16)).reshape(8, 4, 16, 512)
    x_send[...] = cross[...].astype(BF16)
    x_copies = []
    for k in range(1, NX):
        tx = lax.rem(x + k, NX)
        x_copies.append(send(x_send.at[:, tx], x_recv.at[k], x_ss.at[k], x_rs.at[k], device(tx, y, z, h)))
        x_copies[-1].start()
    mine = cross[:, x]
    for k in range(1, NX):
        x_copies[k - 1].wait_recv()
        mine += x_recv[k].astype(F32)
    mine = mine.reshape(8, 2, 8, 512)
    for hi in range(2):
        for lo in range(8):
            piece = mine[lo, hi]
            z_send[hi * 8 + lo] = jnp.concatenate([piece[:, :256], piece[:, 256:]], axis=0).astype(BF16)
    z_copies = []
    for k in range(1, NZ):
        tz = lax.rem(z + k, NZ)
        z_copies.append(send(z_send.at[tz], z_recv.at[k], z_ss.at[k], z_rs.at[k], device(x, y, tz, h)))
        z_copies[-1].start()
    acc = z_send[z].astype(F32)
    for k in range(1, NZ):
        z_copies[k - 1].wait_recv()
        acc += z_recv[k].astype(F32)
    own = square[pl.ds(pl.multiple_of(lax.rem(band * 8, 128), 8), 8), :]
    diag_ref[0, :, :256] = acc[:8] + own[:, :256]
    diag_ref[0, :, 256:] = acc[8:] + own[:, 256:]

    for c in f_copies + a_copies + c_copies + list(ring.values()) + x_copies + z_copies:
        c.wait_send()
    for xx in range(NX):
        here = jnp.logical_and(xx == x, x == y)

        @pl.when(jnp.logical_not(here))
        def _():
            send(o_send.at[xx], o_recv.at[y], o_ss.at[xx], o_rs.at[y], device(xx, x, z, h)).wait_send()

        @pl.when(jnp.logical_and(holds, jnp.logical_not(here)))
        def _():
            send(
                pn.at[lax.rem(z_lo, 2), 2 * xx + z_hi], pd, p_ss.at[xx], p_rs.at[0], device(xx, x, z, h)
            ).wait_send()


def body(ancestor, factor, inv_diag, pattern):
    vmem, dma = pltpu.VMEM, pltpu.SemaphoreType.DMA
    return pl.pallas_call(
        kernel,
        out_shape=(
            jax.ShapeDtypeStruct((1, 128, 512), F32),
            jax.ShapeDtypeStruct((1, 8, 512), F32),
        ),
        in_specs=[
            pl.BlockSpec(memory_space=pltpu.VMEM),
            pl.BlockSpec(memory_space=pltpu.VMEM),
            pl.BlockSpec(memory_space=pl.ANY),
            pl.BlockSpec(memory_space=pltpu.SMEM),
        ],
        out_specs=(pl.BlockSpec(memory_space=pltpu.VMEM), pl.BlockSpec(memory_space=pltpu.VMEM)),
        scratch_shapes=[
            vmem((2, 4, 128, 1024), BF16),
            vmem((2, 4, 16, 512), BF16),
            vmem((2, 8, 4, 2, 16, 512), BF16),
            vmem((512, 512), BF16),
            vmem((512, 512), BF16),
            vmem((128, 512), F32),
            vmem((4, 128, 512), BF16),
            vmem((4, 128, 512), BF16),
            vmem((4, 2, 16, 512), BF16),
            vmem((8, 4, 16, 512), F32),
            vmem((8, 4, 16, 512), BF16),
            vmem((4, 8, 16, 512), BF16),
            vmem((16, 16, 256), BF16),
            vmem((16, 16, 256), BF16),
            dma((8,)), dma((8,)),
            dma((4,)), dma((4,)),
            dma((4,)), dma((4,)),
            dma((2, 8, 2)), dma((2, 8, 2)),
            dma((4,)), dma((4,)),
            dma((4,)), dma((1,)),
            dma((4,)), dma((4,)),
            dma((16,)), dma((16,)),
            dma((2,)),
        ],
        compiler_params=pltpu.CompilerParams(
            collective_id=0, has_side_effects=True, vmem_limit_bytes=48 * 1024 * 1024
        ),
        name="takahashi",
    )(ancestor, factor, inv_diag, pattern)


def solution(mesh):
    return jax.shard_map(
        body,
        mesh=mesh,
        in_specs=(P("row", ("col", "leaf")), P(None, ("row", "col", "leaf"), None), P(), P()),
        out_specs=(P("row", ("col", "leaf"), None), P("row", ("col", "leaf"), None)),
        check_vma=False,
    )
```

time: 1720 us -> 92.1 us (0.05)
  the two profiles are of different devices: /device:TPU:24 before, /device:TPU:8 now
where the time goes in v1:
time: 92.1 us; the launch traced here: 91.9 us
  Pallas kernels  85.2 us (93%)
  local copies, waits for them, and re-layouts  6.03 us (7%)
    pallas_call x1, Pallas kernels, body(): pl.pallas_call(kernel, out_shape=(jax.ShapeDtypeStruct((1, 128, 512), F32...  85.2 us
    unnamed x10, local copies, waits for them, and re-layouts  6.03 us

profile of v1, /device:TPU:8, one launch (start us, length us, event | category | flops | bytes accessed | tf_op | source)
XLA Modules:
  0.0 91.9 jit_solution(1788569665056937686)
XLA Ops:
  0.6 0.0 copy-start
  0.6 2.2 %copy-done = bf16[8,512,512]{2,1,0:T(8,128)(2,1)S(1)} copy-done((bf16[8,512,512]{2,1,0:T(8,128)(2,1)S(1)}, bf16[8,512,512]{2,1,0:T(8,128)(2,1)}, u32[]{:S(2)}) %copy-start) | copy-done | bytes 4194328
  2.8 0.0 copy-start.1
  2.8 0.9 %copy-done.1 = bf16[1024,128]{1,0:T(8,128)(2,1)S(1)} copy-done((bf16[1024,128]{1,0:T(8,128)(2,1)S(1)}, bf16[1024,128]{1,0:T(8,128)(2,1)}, u32[]{:S(2)}) %copy-start.1) | copy-done | bytes 262168
  3.8 0.0 copy-start.2
  3.8 0.9 copy-done.2
  4.7 0.0 copy-start.3
  4.7 0.7 copy-done.3
  5.4 85.2 %takahashi.1 = (f32[1,128,512]{2,1,0:T(8,128)S(1)}, f32[1,8,512]{2,1,0:T(8,128)S(1)}) custom-call(bf16[1024,128]{1,0:T(8,128)(2,1)S(1)} %copy-done.1, bf16[8,16,512]{2,1,0:T(8,128)(2,1)S(1)} %copy-done.2, bf16[8,512,512]{2,1,0:T(8,128)(2,1)S(1)} %copy-done, s32[8,32]{1,0:T(8,128)S(1)} %copy-done.3), custom_call_target="tpu_custom_call" | custom-call | tf_op jit(solution)/shard_map/takahashi/pallas_call | solution.py:234
  90.6 0.7 copy.8
  91.3 0.6 copy.9
Async XLA Ops:
  0.6 2.2 %copy-start = (bf16[8,512,512]{2,1,0:T(8,128)(2,1)S(1)}, bf16[8,512,512]{2,1,0:T(8,128)(2,1)}, u32[]{:S(2)}) copy-start(bf16[8,512,512]{2,1,0:T(8,128)(2,1)} %inv_ref.1) | copy-start | bytes 12582916
  2.8 0.9 %copy-start.1 = (bf16[1024,128]{1,0:T(8,128)(2,1)S(1)}, bf16[1024,128]{1,0:T(8,128)(2,1)}, u32[]{:S(2)}) copy-start(bf16[1024,128]{1,0:T(8,128)(2,1)} %a_ref.1) | copy-start | bytes 786436
  3.8 0.9 copy-start.2
  4.7 0.7 copy-start.3

commit v2 on v1

v2 whole, which is shorter than its diff:
```python
import functools

import jax
import jax.numpy as jnp
from jax import lax
from jax.experimental import pallas as pl
from jax.experimental.pallas import tpu as pltpu
from jax.sharding import PartitionSpec as P

MESH = pl.DeviceIdType.MESH
NX, NY, NZ, ZLO = 4, 4, 16, 8
F32, BF16 = jnp.float32, jnp.bfloat16


def device(x, y, z, h):
    return (2 * y + h, 4 * lax.rem(z, ZLO) + x, z // ZLO)


def contract_rows(a, b):
    return lax.dot_general(a, b, (((0,), (0,)), ((), ())), preferred_element_type=F32)


def both(*conditions):
    return functools.reduce(jnp.logical_and, conditions)


def kernel(
    a_hbm, factor_hbm, inv_hbm, pattern_hbm, out_ref, diag_ref,
    a_ref, factor_ref, pattern_ref, at, fbuf, pn, pc, inv_own, inv_sq, square, part, y_send, y_recv,
    o_send, o_recv, z_send, z_recv,
    f_ss, f_rs, a_ss, a_rs, c_ss, c_rs, r_ss, r_rs, p_ss, p_rs, y_ss, y_rs, o_ss, o_rs, z_ss, z_rs, l_sem,
):
    row, col, z_hi = lax.axis_index("row"), lax.axis_index("col"), lax.axis_index("leaf")
    y, h = row // 2, lax.rem(row, 2)
    z_lo, x = col // 4, lax.rem(col, 4)
    z = z_hi * ZLO + z_lo
    band = col * 2 + z_hi
    child = 2 * x + h

    def send(src, dst, ss, rs, to):
        return pltpu.make_async_remote_copy(
            src_ref=src, dst_ref=dst, send_sem=ss, recv_sem=rs, device_id=to, device_id_type=MESH
        )

    loads = [
        pltpu.make_async_copy(src, dst, l_sem.at[i])
        for i, (src, dst) in enumerate((
            (factor_hbm, factor_ref), (a_hbm, a_ref), (pattern_hbm, pattern_ref),
            (inv_hbm.at[child], inv_own), (inv_hbm.at[row], inv_sq),
        ))
    ]
    for c in loads:
        c.start()

    barrier = pltpu.get_barrier_semaphore()

    def greet(to):
        pl.semaphore_signal(barrier, inc=1, device_id=to, device_id_type=MESH)

    for k in range(1, 8):
        greet(device(lax.rem(x + k // 2, NX), y, z, lax.rem(h + k % 2, 2)))
    for k in (1, NZ - 1):
        greet(device(x, y, lax.rem(z + k, NZ), h))
    for k in range(1, NY):
        greet(device(x, lax.rem(y + k, NY), z, h))
    loads[0].wait()
    pl.semaphore_wait(barrier, 12)

    f_copies = []
    for k in range(1, 8):
        tx, th = lax.rem(x + k // 2, NX), lax.rem(h + k % 2, 2)
        f_copies.append(
            send(factor_ref.at[2 * tx + th], fbuf.at[h, x], f_ss.at[k], f_rs.at[k], device(tx, y, z, th))
        )
        f_copies[-1].start()
    fbuf[h, x] = factor_ref[child]

    loads[1].wait()
    at[h, x] = a_ref[...].T
    a_copies = []
    for k in range(1, NX):
        a_copies.append(
            send(at.at[h, x], at.at[h, x], a_ss.at[k], a_rs.at[k], device(lax.rem(x + k, NX), y, z, h))
        )
        a_copies[-1].start()
    c_copies = []

    def to_sibling(k):
        sx = lax.rem(x + NX - k, NX)
        if k:
            a_copies[k - 1].wait_recv()
        c_copies.append(send(at.at[h, sx], at.at[h, sx], c_ss.at[k], c_rs.at[k], device(x, y, z, 1 - h)))
        c_copies[-1].start()

    to_sibling(0)

    for c in loads[2:4]:
        c.wait()
    for c in f_copies:
        c.wait_recv()
    pieces = []
    for hh in range(2):
        keep = pattern_ref[child, 4 * (2 * y + hh) + z_lo // 2]
        pieces.append((fbuf[hh].reshape(64, 512).astype(F32) * keep.astype(F32)).astype(BF16))
    masked = jnp.concatenate(pieces, axis=0)
    panel = jnp.dot(masked, inv_own[...], preferred_element_type=F32).astype(BF16).reshape(2, 4, 16, 512)
    for hh in range(2):
        for xx in range(4):
            pn[hh, z_lo, xx, z_hi] = panel[hh, xx]

    holds = y == z_lo // 2

    def share(zz, hh):
        @pl.when(both(holds, lax.rem(z_lo, 2) == hh, lax.rem(zz, 2) == z_hi))
        def _():
            zl, zh = lax.rem(zz, ZLO), zz // ZLO
            for k in (1, 3, 2):
                send(
                    pn.at[hh, zl, :, zh], pc.at[zl // 2, :, zh], p_ss.at[zl // 2, zh, k], p_rs.at[zl // 2, zh],
                    device(x, lax.rem(y + k, NY), z, h),
                ).start()
            pc[zl // 2, :, zh] = pn[hh, zl, :, zh]

    def shard(zz, s):
        return pn.at[s // 2, lax.rem(zz, ZLO), pl.ds(s % 2 * 2, 2), zz // ZLO]

    ring = {}
    for t in range(1, 9):
        for s in range(4):
            for d in range(2):
                src = lax.rem(z + (NZ - (t - 1) if d == 0 else t - 1), NZ)
                to = lax.rem(z + (1 if d == 0 else NZ - 1), NZ)
                if t > 1:
                    ring[d, t - 1, s].wait_recv()
                if t < 8 or d == s // 2:
                    ring[d, t, s] = send(
                        shard(src, s), shard(src, s), r_ss.at[d, t - 1, s], r_rs.at[d, t - 1, s],
                        device(x, y, to, h),
                    )
                    ring[d, t, s].start()
                if s % 2 == 1 and (t > 1 or d == 0):
                    share(src, s // 2)
        if t == 1:
            loads[4].wait()
            lanes = pl.multiple_of((band * 8) // 128 * 128, 128)
            square[...] = contract_rows(inv_sq[:, pl.ds(lanes, 128)], inv_sq[...])
        if t == 6:
            to_sibling(1)
            to_sibling(3)
        if t == 7:
            to_sibling(2)
    for s in range(4):
        ring[s // 2, 8, s].wait_recv()
        if s % 2 == 1:
            share(lax.rem(z + 8, NZ), s // 2)

    for c in c_copies:
        c.wait_recv()
    for xx in range(NX):
        block = jnp.dot(at[0, xx], pn[0].reshape(1024, 512), preferred_element_type=F32)
        block += jnp.dot(at[1, xx], pn[1].reshape(1024, 512), preferred_element_type=F32)
        for yy in range(NY):
            columns = block[:, yy * 128 : yy * 128 + 128]
            part[yy, xx] = columns
            y_send[yy, xx] = columns.astype(BF16)
    y_copies = []
    for k in range(1, NY):
        ty = lax.rem(y + k, NY)
        y_copies.append(send(y_send.at[ty], y_recv.at[k], y_ss.at[k], y_rs.at[k], device(x, ty, z, h)))
        y_copies[-1].start()
    total = part[y]
    for k in range(1, NY):
        y_copies[k - 1].wait_recv()
        total += y_recv[k].astype(F32)

    o_send[...] = total
    for xx in range(NX):
        here = both(xx == x, x == y)

        @pl.when(jnp.logical_not(here))
        def _():
            send(o_send.at[xx], o_recv.at[y], o_ss.at[xx], o_rs.at[y], device(xx, x, z, h)).start()

        @pl.when(here)
        def _():
            o_recv[y] = o_send[xx]

    @pl.when(jnp.logical_not(holds))
    def _():
        for i in range(4):
            for zh in range(2):
                send(
                    pn.at[0, 0, :, 0], pc.at[i, :, zh], p_ss.at[i, zh, 0], p_rs.at[i, zh], device(x, y, z, 1 - h)
                ).wait_recv()

    cross = contract_rows(total.astype(BF16).reshape(512, 128), pc[...].reshape(512, 512)).reshape(16, 8, 512)
    for i in range(16):
        z_send[i] = jnp.concatenate([cross[i][:, :256], cross[i][:, 256:]], axis=0).astype(BF16)

    def piece(i):
        tx, tz = lax.rem(i // 2, 4), lax.rem(i, 2) * ZLO + 2 * y + i // 8
        return device(tx, x, tz, h), both(tx == x, x == y, tz == z)

    for n in range(16):
        i = lax.rem(z + n, 16)
        to, here = piece(i)

        @pl.when(jnp.logical_not(here))
        def _():
            send(z_send.at[i], z_recv.at[z], z_ss.at[i], z_rs.at[z], to).start()

        @pl.when(here)
        def _():
            z_recv[z] = z_send[i]

    keep = -pattern_ref[row, col].astype(F32)
    for yy in range(NY):

        @pl.when(jnp.logical_not(both(x == y, yy == y)))
        def _():
            send(o_send.at[0], o_recv.at[yy], o_ss.at[0], o_rs.at[yy], device(x, y, z, 1 - h)).wait_recv()

        out_ref[0, :, yy * 128 : yy * 128 + 128] = o_recv[yy] * keep
    for zz in range(NZ):

        @pl.when(jnp.logical_not(both(x == y, holds, zz == z)))
        def _():
            send(z_send.at[0], z_recv.at[zz], z_ss.at[0], z_rs.at[zz], device(x, y, z, 1 - h)).wait_recv()

    acc = z_recv[0].astype(F32)
    for zz in range(1, NZ):
        acc += z_recv[zz].astype(F32)
    own = square[pl.ds(pl.multiple_of(lax.rem(band * 8, 128), 8), 8), :]
    diag_ref[0, :, :256] = acc[:8] + own[:, :256]
    diag_ref[0, :, 256:] = acc[8:] + own[:, 256:]

    for c in f_copies + a_copies + c_copies + list(ring.values()) + y_copies:
        c.wait_send()

    @pl.when(holds)
    def _():
        for i in range(4):
            for zh in range(2):
                for k in (1, 2, 3):
                    send(
                        pn.at[0, 0, :, 0], pc.at[i, :, zh], p_ss.at[i, zh, k], p_rs.at[i, zh],
                        device(x, lax.rem(y + k, NY), z, h),
                    ).wait_send()

    for xx in range(NX):

        @pl.when(jnp.logical_not(both(xx == x, x == y)))
        def _():
            send(o_send.at[xx], o_recv.at[y], o_ss.at[xx], o_rs.at[y], device(xx, x, z, h)).wait_send()

    for i in range(16):
        to, here = piece(i)

        @pl.when(jnp.logical_not(here))
        def _():
            send(z_send.at[i], z_recv.at[z], z_ss.at[i], z_rs.at[z], to).wait_send()


def body(ancestor, factor, inv_diag, pattern):
    vmem, dma = pltpu.VMEM, pltpu.SemaphoreType.DMA
    return pl.pallas_call(
        kernel,
        out_shape=(
            jax.ShapeDtypeStruct((1, 128, 512), F32),
            jax.ShapeDtypeStruct((1, 8, 512), F32),
        ),
        in_specs=[pl.BlockSpec(memory_space=pl.ANY)] * 4,
        out_specs=(pl.BlockSpec(memory_space=pltpu.VMEM), pl.BlockSpec(memory_space=pltpu.VMEM)),
        scratch_shapes=[
            vmem((1024, 128), BF16),
            vmem((8, 16, 512), BF16),
            pltpu.SMEM((8, 32), jnp.int32),
            vmem((2, 4, 128, 1024), BF16),
            vmem((2, 4, 16, 512), BF16),
            vmem((2, 8, 4, 2, 16, 512), BF16),
            vmem((4, 4, 2, 16, 512), BF16),
            vmem((512, 512), BF16),
            vmem((512, 512), BF16),
            vmem((128, 512), F32),
            vmem((4, 4, 128, 128), F32),
            vmem((4, 4, 128, 128), BF16),
            vmem((4, 4, 128, 128), BF16),
            vmem((4, 128, 128), F32),
            vmem((4, 128, 128), F32),
            vmem((16, 16, 256), BF16),
            vmem((16, 16, 256), BF16),
            dma((8,)), dma((8,)),
            dma((4,)), dma((4,)),
            dma((4,)), dma((4,)),
            dma((2, 8, 4)), dma((2, 8, 4)),
            dma((4, 2, 4)), dma((4, 2)),
            dma((4,)), dma((4,)),
            dma((4,)), dma((4,)),
            dma((16,)), dma((16,)),
            dma((5,)),
        ],
        compiler_params=pltpu.CompilerParams(
            collective_id=0, has_side_effects=True, vmem_limit_bytes=60 * 1024 * 1024
        ),
        name="takahashi",
    )(ancestor, factor, inv_diag, pattern)


def solution(mesh):
    return jax.shard_map(
        body,
        mesh=mesh,
        in_specs=(P("row", ("col", "leaf")), P(None, ("row", "col", "leaf"), None), P(), P()),
        out_specs=(P("row", ("col", "leaf"), None), P("row", ("col", "leaf"), None)),
        check_vma=False,
    )
```

time: 92.1 us -> 78.5 us (0.85)
  the two profiles are of different devices: /device:TPU:8 before, /device:TPU:24 now
where the time goes in v2:
time: 78.5 us; the launch traced here: 78.1 us
  Pallas kernels  74.5 us (95%)
  local copies, waits for them, and re-layouts  2.99 us (4%)
    pallas_call x1, Pallas kernels, body(): pl.pallas_call(kernel, out_shape=(jax.ShapeDtypeStruct((1, 128, 512), F32...  74.5 us
    unnamed x2, local copies, waits for them, and re-layouts  2.99 us

profile of v2, /device:TPU:24, one launch (start us, length us, event | category | flops | bytes accessed | tf_op | source)
XLA Modules:
  0.0 78.1 jit_solution(5573118925382584420)
XLA Ops:
  0.6 74.5 %takahashi.1 = (f32[1,128,512]{2,1,0:T(8,128)}, f32[1,8,512]{2,1,0:T(8,128)}) custom-call(bf16[1024,128]{1,0:T(8,128)(2,1)} %a_hbm.1, bf16[8,16,512]{2,1,0:T(8,128)(2,1)} %factor_hbm.1, bf16[8,512,512]{2,1,0:T(8,128)(2,1)} %inv_hbm.1, s32[8,32]{1,0:T(8,128)} %pattern_hbm.1), custom_call_target="tpu_custom_call" | custom-call | tf_op jit(solution)/shard_map/takahashi/pallas_call | solution.py:266
  75.1 1.7 %copy.8 = f32[1,128,512]{2,1,0:T(8,128)} copy(f32[1,128,512]{2,1,0:T(8,128)} %get-tuple-element.4) | data formatting | bytes 524288
  76.8 1.3 %copy.9 = f32[1,8,512]{2,1,0:T(8,128)} copy(f32[1,8,512]{2,1,0:T(8,128)} %get-tuple-element.5) | data formatting | bytes 32768

commit v3 on v2

--- a/solution.py
+++ b/solution.py
@@ -75,14 +75,7 @@
         f_copies[-1].start()
     fbuf[h, x] = factor_ref[child]
 
-    loads[1].wait()
-    at[h, x] = a_ref[...].T
     a_copies = []
-    for k in range(1, NX):
-        a_copies.append(
-            send(at.at[h, x], at.at[h, x], a_ss.at[k], a_rs.at[k], device(lax.rem(x + k, NX), y, z, h))
-        )
-        a_copies[-1].start()
     c_copies = []
 
     def to_sibling(k):
@@ -91,8 +84,6 @@
             a_copies[k - 1].wait_recv()
         c_copies.append(send(at.at[h, sx], at.at[h, sx], c_ss.at[k], c_rs.at[k], device(x, y, z, 1 - h)))
         c_copies[-1].start()
-
-    to_sibling(0)
 
     for c in loads[2:4]:
         c.wait()
@@ -141,6 +132,14 @@
                 if s % 2 == 1 and (t > 1 or d == 0):
                     share(src, s // 2)
         if t == 1:
+            loads[1].wait()
+            at[h, x] = a_ref[...].T
+            for k in range(1, NX):
+                a_copies.append(
+                    send(at.at[h, x], at.at[h, x], a_ss.at[k], a_rs.at[k], device(lax.rem(x + k, NX), y, z, h))
+                )
+                a_copies[-1].start()
+            to_sibling(0)
             loads[4].wait()
             lanes = pl.multiple_of((band * 8) // 128 * 128, 128)
             square[...] = contract_rows(inv_sq[:, pl.ds(lanes, 128)], inv_sq[...])

time: 78.5 us -> 72.7 us (0.926)
  Pallas kernels: 74.5 us -> 68.5 us
    pallas_call x1, Pallas kernels: 74.5 us -> 68.5 us  [body(): pl.pallas_call(kernel, out_shape=(jax.ShapeDtypeStruct((1, 128, 512), F32...]
where the time goes in v3:
time: 72.7 us; the launch traced here: 72.2 us
  Pallas kernels  68.5 us (94%)
  local copies, waits for them, and re-layouts  2.99 us (4%)
    pallas_call x1, Pallas kernels, body(): pl.pallas_call(kernel, out_shape=(jax.ShapeDtypeStruct((1, 128, 512), F32...  68.5 us
    unnamed x2, local copies, waits for them, and re-layouts  2.99 us

profile of v3, /device:TPU:24, one launch (start us, length us, event | category | flops | bytes accessed | tf_op | source)
XLA Modules:
  0.0 72.2 jit_solution(15708697195387891097)
XLA Ops:
  0.6 68.5 %takahashi.1 = (f32[1,128,512]{2,1,0:T(8,128)}, f32[1,8,512]{2,1,0:T(8,128)}) custom-call(bf16[1024,128]{1,0:T(8,128)(2,1)} %a_hbm.1, bf16[8,16,512]{2,1,0:T(8,128)(2,1)} %factor_hbm.1, bf16[8,512,512]{2,1,0:T(8,128)(2,1)} %inv_hbm.1, s32[8,32]{1,0:T(8,128)} %pattern_hbm.1), custom_call_target="tpu_custom_call" | custom-call | tf_op jit(solution)/shard_map/takahashi/pallas_call | solution.py:265
  69.2 1.7 %copy.8 = f32[1,128,512]{2,1,0:T(8,128)} copy(f32[1,128,512]{2,1,0:T(8,128)} %get-tuple-element.4) | data formatting | bytes 524288
  70.8 1.3 %copy.9 = f32[1,8,512]{2,1,0:T(8,128)} copy(f32[1,8,512]{2,1,0:T(8,128)} %get-tuple-element.5) | data formatting | bytes 32768

commit v4 on v3

v4 whole, which is shorter than its diff:
```python
import functools

import jax
import jax.numpy as jnp
from jax import lax
from jax.experimental import pallas as pl
from jax.experimental.pallas import tpu as pltpu
from jax.sharding import PartitionSpec as P

MESH = pl.DeviceIdType.MESH
NX, NY, NZ, ZLO = 4, 4, 16, 8
F32, BF16 = jnp.float32, jnp.bfloat16


def device(x, y, z, h):
    return (2 * y + h, 4 * lax.rem(z, ZLO) + x, z // ZLO)


def contract_rows(a, b):
    return lax.dot_general(a, b, (((0,), (0,)), ((), ())), preferred_element_type=F32)


def both(*conditions):
    return functools.reduce(jnp.logical_and, conditions)


def kernel(
    a_hbm, factor_hbm, inv_hbm, pattern_hbm, out_hbm, diag_hbm,
    out_ref, diag_ref,    a_ref, factor_ref, pattern_ref, at, fbuf, pn, pc, inv_own, inv_sq, square, part, y_send, y_recv,
    o_send, o_recv, z_send, z_recv,
    f_ss, f_rs, a_ss, a_rs, c_ss, c_rs, r_ss, r_rs, p_ss, p_rs, y_ss, y_rs, o_ss, o_rs, z_ss, z_rs, l_sem,
):
    row, col, z_hi = lax.axis_index("row"), lax.axis_index("col"), lax.axis_index("leaf")
    y, h = row // 2, lax.rem(row, 2)
    z_lo, x = col // 4, lax.rem(col, 4)
    z = z_hi * ZLO + z_lo
    band = col * 2 + z_hi
    child = 2 * x + h

    def send(src, dst, ss, rs, to):
        return pltpu.make_async_remote_copy(
            src_ref=src, dst_ref=dst, send_sem=ss, recv_sem=rs, device_id=to, device_id_type=MESH
        )

    def all_in(like, sem):
        pltpu.make_async_copy(like, like, sem).wait()

    def most(one_here, like, count, sem):
        for fewer in range(2):

            @pl.when(one_here if fewer else jnp.logical_not(one_here))
            def _():
                all_in(like.at[pl.ds(0, count - fewer)], sem)

    loads = [
        pltpu.make_async_copy(src, dst, l_sem.at[i])
        for i, (src, dst) in enumerate((
            (factor_hbm, factor_ref), (a_hbm, a_ref), (pattern_hbm, pattern_ref),
            (inv_hbm.at[child], inv_own), (inv_hbm.at[row], inv_sq),
        ))
    ]
    for c in loads:
        c.start()

    barrier = pltpu.get_barrier_semaphore()

    def greet(to):
        pl.semaphore_signal(barrier, inc=1, device_id=to, device_id_type=MESH)

    for k in range(1, 8):
        greet(device(lax.rem(x + k // 2, NX), y, z, lax.rem(h + k % 2, 2)))
    for k in (1, NZ - 1):
        greet(device(x, y, lax.rem(z + k, NZ), h))
    for k in range(1, NY):
        greet(device(x, lax.rem(y + k, NY), z, h))
    loads[0].wait()
    pl.semaphore_wait(barrier, 12)

    for k in range(1, 8):
        tx, th = lax.rem(x + k // 2, NX), lax.rem(h + k % 2, 2)
        send(factor_ref.at[2 * tx + th], fbuf.at[h, x], f_ss, f_rs, device(tx, y, z, th)).start()
    fbuf[h, x] = factor_ref[child]

    for c in loads[2:4]:
        c.wait()
    all_in(factor_ref.at[pl.ds(0, 7)], f_rs)
    pieces = []
    for hh in range(2):
        keep = pattern_ref[child, 4 * (2 * y + hh) + z_lo // 2]
        pieces.append((fbuf[hh].reshape(64, 512).astype(F32) * keep.astype(F32)).astype(BF16))
    masked = jnp.concatenate(pieces, axis=0)
    panel = jnp.dot(masked, inv_own[...], preferred_element_type=F32).astype(BF16).reshape(2, 4, 16, 512)
    for hh in range(2):
        for xx in range(4):
            pn[hh, z_lo, xx, z_hi] = panel[hh, xx]

    holds = y == z_lo // 2

    def share(zz, hh):
        @pl.when(both(holds, lax.rem(z_lo, 2) == hh, lax.rem(zz, 2) == z_hi))
        def _():
            zl, zh = lax.rem(zz, ZLO), zz // ZLO
            for k in (1, 3, 2):
                send(
                    pn.at[hh, zl, :, zh], pc.at[zl // 2, :, zh], p_ss, p_rs,
                    device(x, lax.rem(y + k, NY), z, h),
                ).start()
            pc[zl // 2, :, zh] = pn[hh, zl, :, zh]

    def shard(zz, s):
        return pn.at[s // 2, lax.rem(zz, ZLO), pl.ds(s % 2 * 2, 2), zz // ZLO]

    ring = {}
    for t in range(1, 9):
        for s in range(4):
            for d in range(2):
                src = lax.rem(z + (NZ - (t - 1) if d == 0 else t - 1), NZ)
                to = lax.rem(z + (1 if d == 0 else NZ - 1), NZ)
                if t > 1:
                    ring[d, t - 1, s].wait_recv()
                if t < 8 or d == s // 2:
                    ring[d, t, s] = send(
                        shard(src, s), shard(src, s), r_ss.at[(t - 1) // 4 + t // 8], r_rs.at[d, t - 1, s],
                        device(x, y, to, h),
                    )
                    ring[d, t, s].start()
                if s % 2 == 1 and (t > 1 or d == 0):
                    share(src, s // 2)
        if t == 1:
            loads[1].wait()
            at[h, x] = a_ref[...].T
            for k in (1, 3, 2):
                send(at.at[h, x], at.at[h, x], a_ss, a_rs, device(lax.rem(x + k, NX), y, z, h)).start()
            loads[4].wait()
            lanes = pl.multiple_of((band * 8) // 128 * 128, 128)
            square[...] = contract_rows(inv_sq[:, pl.ds(lanes, 128)], inv_sq[...])
        if t == 7:
            all_in(at.at[0, pl.ds(0, 3)], a_rs)
            for k in range(NX):
                send(at.at[h, k], at.at[h, k], c_ss, c_rs, device(x, y, z, 1 - h)).start()
    for s in range(4):
        ring[s // 2, 8, s].wait_recv()
        if s % 2 == 1:
            share(lax.rem(z + 8, NZ), s // 2)

    all_in(at.at[0], c_rs)
    for xx in range(NX):
        block = jnp.dot(at[0, xx], pn[0].reshape(1024, 512), preferred_element_type=F32)
        block += jnp.dot(at[1, xx], pn[1].reshape(1024, 512), preferred_element_type=F32)
        for yy in range(NY):
            columns = block[:, yy * 128 : yy * 128 + 128]
            part[yy, xx] = columns
            y_send[yy, xx] = columns.astype(BF16)
    for k in range(1, NY):
        ty = lax.rem(y + k, NY)
        send(y_send.at[ty], y_recv.at[k], y_ss, y_rs.at[k - 1], device(x, ty, z, h)).start()
    total = part[y]
    for k in range(1, NY):
        all_in(y_recv.at[k], y_rs.at[k - 1])
        total += y_recv[k].astype(F32)

    o_send[...] = total
    for xx in range(NX):
        here = both(xx == x, x == y)

        @pl.when(jnp.logical_not(here))
        def _():
            send(o_send.at[xx], o_recv.at[y], o_ss, o_rs, device(xx, x, z, h)).start()

        @pl.when(here)
        def _():
            o_recv[y] = o_send[xx]

    @pl.when(jnp.logical_not(holds))
    def _():
        all_in(pc, p_rs)

    cross = contract_rows(total.astype(BF16).reshape(512, 128), pc[...].reshape(512, 512)).reshape(16, 8, 512)
    for i in range(16):
        z_send[i] = jnp.concatenate([cross[i][:, :256], cross[i][:, 256:]], axis=0).astype(BF16)

    def piece(i):
        tx, tz = lax.rem(i // 2, 4), lax.rem(i, 2) * ZLO + 2 * y + i // 8
        return device(tx, x, tz, h), both(tx == x, x == y, tz == z)

    for n in range(16):
        i = lax.rem(z + n, 16)
        to, here = piece(i)

        @pl.when(jnp.logical_not(here))
        def _():
            send(z_send.at[i], z_recv.at[z], z_ss, z_rs, to).start()

        @pl.when(here)
        def _():
            z_recv[z] = z_send[i]

    keep = -pattern_ref[row, col].astype(F32)
    most(x == y, o_recv, NX, o_rs)
    for yy in range(NY):
        out_ref[0, :, yy * 128 : yy * 128 + 128] = o_recv[yy] * keep
    out_copy = pltpu.make_async_copy(out_ref, out_hbm, l_sem.at[0])
    out_copy.start()
    most(both(x == y, holds), z_recv, NZ, z_rs)
    acc = z_recv[0].astype(F32)
    for zz in range(1, NZ):
        acc += z_recv[zz].astype(F32)
    own = square[pl.ds(pl.multiple_of(lax.rem(band * 8, 128), 8), 8), :]
    diag_ref[0, :, :256] = acc[:8] + own[:, :256]
    diag_ref[0, :, 256:] = acc[8:] + own[:, 256:]

    diag_copy = pltpu.make_async_copy(diag_ref, diag_hbm, l_sem.at[1])
    diag_copy.start()
    out_copy.wait()

    all_in(factor_ref.at[pl.ds(0, 7)], f_ss)
    all_in(at.at[0, pl.ds(0, 3)], a_ss)
    all_in(at.at[0], c_ss)
    all_in(pn.at[0], r_ss.at[0])
    all_in(pn.at[:, pl.ds(0, 6), :, 0], r_ss.at[1])
    all_in(pn.at[0, 0], r_ss.at[2])
    all_in(y_send.at[pl.ds(0, 3)], y_ss)
    most(x == y, o_send, NX, o_ss)

    @pl.when(holds)
    def _():
        all_in(pn.at[:, pl.ds(0, 6)], p_ss)

    most(both(x == y, holds), z_send, NZ, z_ss)
    diag_copy.wait()


def deliver(panel_ref, diag_ref, panel_out, diag_out):
    panel_out[...] = panel_ref[...]
    diag_out[...] = diag_ref[...]


def body(ancestor, factor, inv_diag, pattern):
    vmem, dma = pltpu.VMEM, pltpu.SemaphoreType.DMA
    results = pl.pallas_call(
        kernel,
        out_shape=(
            jax.ShapeDtypeStruct((1, 128, 512), F32),
            jax.ShapeDtypeStruct((1, 8, 512), F32),
        ),
        in_specs=[pl.BlockSpec(memory_space=pl.ANY)] * 4,
        out_specs=(pl.BlockSpec(memory_space=pl.ANY), pl.BlockSpec(memory_space=pl.ANY)),
        scratch_shapes=[
            vmem((1, 128, 512), F32),
            vmem((1, 8, 512), F32),
            vmem((1024, 128), BF16),
            vmem((8, 16, 512), BF16),
            pltpu.SMEM((8, 32), jnp.int32),
            vmem((2, 4, 128, 1024), BF16),
            vmem((2, 4, 16, 512), BF16),
            vmem((2, 8, 4, 2, 16, 512), BF16),
            vmem((4, 4, 2, 16, 512), BF16),
            vmem((512, 512), BF16),
            vmem((512, 512), BF16),
            vmem((128, 512), F32),
            vmem((4, 4, 128, 128), F32),
            vmem((4, 4, 128, 128), BF16),
            vmem((4, 4, 128, 128), BF16),
            vmem((4, 128, 128), F32),
            vmem((4, 128, 128), F32),
            vmem((16, 16, 256), BF16),
            vmem((16, 16, 256), BF16),
            dma, dma,
            dma, dma,
            dma, dma,
            dma((3,)), dma((2, 8, 4)),
            dma, dma,
            dma, dma((3,)),
            dma, dma,
            dma, dma,
            dma((5,)),
        ],
        compiler_params=pltpu.CompilerParams(
            collective_id=0, has_side_effects=True, vmem_limit_bytes=60 * 1024 * 1024
        ),
        name="takahashi",
    )(ancestor, factor, inv_diag, pattern)
    return pl.pallas_call(
        deliver,
        out_shape=tuple(jax.ShapeDtypeStruct(r.shape, F32) for r in results),
        in_specs=[pl.BlockSpec(memory_space=pltpu.VMEM)] * 2,
        out_specs=(pl.BlockSpec(memory_space=pltpu.VMEM), pl.BlockSpec(memory_space=pltpu.VMEM)),
        compiler_params=pltpu.CompilerParams(vmem_limit_bytes=60 * 1024 * 1024),
        name="deliver",
    )(*results)


def solution(mesh):
    return jax.shard_map(
        body,
        mesh=mesh,
        in_specs=(P("row", ("col", "leaf")), P(None, ("row", "col", "leaf"), None), P(), P()),
        out_specs=(P("row", ("col", "leaf"), None), P("row", ("col", "leaf"), None)),
        check_vma=False,
    )
```

time: 72.7 us -> 69.4 us (0.955)
  local copies, waits for them, and re-layouts: 2.99 us -> 0 us
    unnamed x2 -> x0, local copies, waits for them, and re-layouts: 2.99 us -> none
    pallas_call x0 -> x1, Pallas kernels: none -> 1.68 us  [body(): pl.pallas_call(deliver, out_shape=tuple((jax.ShapeDtypeStruct(r.shape, F3...]
    pallas_call x1, Pallas kernels: 68.5 us -> 66.9 us  [body(): pl.pallas_call(kernel, out_shape=(jax.ShapeDtypeStruct((1, 128, 512), F32...]
where the time goes in v4:
time: 69.4 us; the launch traced here: 69.3 us
  Pallas kernels  68.6 us (99%)
    pallas_call x1, Pallas kernels, body(): pl.pallas_call(kernel, out_shape=(jax.ShapeDtypeStruct((1, 128, 512), F32...  66.9 us
    pallas_call x1, Pallas kernels, body(): pl.pallas_call(deliver, out_shape=tuple((jax.ShapeDtypeStruct(r.shape, F3...  1.68 us

profile of v4, /device:TPU:24, one launch (start us, length us, event | category | flops | bytes accessed | tf_op | source)
XLA Modules:
  0.0 69.3 jit_solution(12248743092334532104)
XLA Ops:
  0.6 66.9 %takahashi.1 = (f32[1,128,512]{2,1,0:T(8,128)}, f32[1,8,512]{2,1,0:T(8,128)}) custom-call(bf16[1024,128]{1,0:T(8,128)(2,1)} %a_hbm.1, bf16[8,16,512]{2,1,0:T(8,128)(2,1)} %factor_hbm.1, bf16[8,512,512]{2,1,0:T(8,128)(2,1)} %inv_hbm.1, s32[8,32]{1,0:T(8,128)} %pattern_hbm.1), custom_call_target="tpu_custom_call" | custom-call | tf_op jit(solution)/shard_map/takahashi/pallas_call | solution.py:240
  67.6 1.7 %deliver.1 = (f32[1,128,512]{2,1,0:T(8,128)}, f32[1,8,512]{2,1,0:T(8,128)}) custom-call(f32[1,128,512]{2,1,0:T(8,128)} %get-tuple-element.4.panel_ref, f32[1,8,512]{2,1,0:T(8,128)} %get-tuple-element.5.diag_ref), custom_call_target="tpu_custom_call" | custom-call | tf_op jit(solution)/shard_map/deliver/pallas_call | solution.py:283

commit v5 on v4

--- a/solution.py
+++ b/solution.py
@@ -26,7 +26,7 @@
 
 def kernel(
     a_hbm, factor_hbm, inv_hbm, pattern_hbm, out_hbm, diag_hbm,
-    out_ref, diag_ref,    a_ref, factor_ref, pattern_ref, at, fbuf, pn, pc, inv_own, inv_sq, square, part, y_send, y_recv,
+    out_ref, diag_ref,    a_ref, factor_ref, pattern_ref, at, fbuf, pn, pc, inv_own, inv_sq, square, part, y_send, y_recv, rounded,
     o_send, o_recv, z_send, z_recv,
     f_ss, f_rs, a_ss, a_rs, c_ss, c_rs, r_ss, r_rs, p_ss, p_rs, y_ss, y_rs, o_ss, o_rs, z_ss, z_rs, l_sem,
 ):
@@ -151,15 +151,21 @@
             columns = block[:, yy * 128 : yy * 128 + 128]
             part[yy, xx] = columns
             y_send[yy, xx] = columns.astype(BF16)
-    for k in range(1, NY):
-        ty = lax.rem(y + k, NY)
-        send(y_send.at[ty], y_recv.at[k], y_ss, y_rs.at[k - 1], device(x, ty, z, h)).start()
-    total = part[y]
-    for k in range(1, NY):
-        all_in(y_recv.at[k], y_rs.at[k - 1])
-        total += y_recv[k].astype(F32)
-
-    o_send[...] = total
+        if xx % 2 == 1:
+            for k in range(1, NY):
+                ty, half = lax.rem(y + k, NY), pl.ds(xx - 1, 2)
+                send(
+                    y_send.at[ty, half], y_recv.at[k, half], y_ss, y_rs.at[k - 1, xx // 2], device(x, ty, z, h)
+                ).start()
+    for half in range(2):
+        pair = pl.ds(2 * half, 2)
+        total = part[y, pair]
+        for k in range(1, NY):
+            all_in(y_recv.at[k, pair], y_rs.at[k - 1, half])
+            total += y_recv[k, pair].astype(F32)
+        o_send[pair] = total.astype(o_send.dtype)
+        rounded[pair] = total.astype(BF16)
+
     for xx in range(NX):
         here = both(xx == x, x == y)
 
@@ -175,7 +181,7 @@
     def _():
         all_in(pc, p_rs)
 
-    cross = contract_rows(total.astype(BF16).reshape(512, 128), pc[...].reshape(512, 512)).reshape(16, 8, 512)
+    cross = contract_rows(rounded[...].reshape(512, 128), pc[...].reshape(512, 512)).reshape(16, 8, 512)
     for i in range(16):
         z_send[i] = jnp.concatenate([cross[i][:, :256], cross[i][:, 256:]], axis=0).astype(BF16)
 
@@ -198,7 +204,7 @@
     keep = -pattern_ref[row, col].astype(F32)
     most(x == y, o_recv, NX, o_rs)
     for yy in range(NY):
-        out_ref[0, :, yy * 128 : yy * 128 + 128] = o_recv[yy] * keep
+        out_ref[0, :, yy * 128 : yy * 128 + 128] = o_recv[yy].astype(F32) * keep
     out_copy = pltpu.make_async_copy(out_ref, out_hbm, l_sem.at[0])
     out_copy.start()
     most(both(x == y, holds), z_recv, NZ, z_rs)
@@ -261,8 +267,9 @@
             vmem((4, 4, 128, 128), F32),
             vmem((4, 4, 128, 128), BF16),
             vmem((4, 4, 128, 128), BF16),
-            vmem((4, 128, 128), F32),
-            vmem((4, 128, 128), F32),
+            vmem((4, 128, 128), BF16),
+            vmem((4, 128, 128), BF16),
+            vmem((4, 128, 128), BF16),
             vmem((16, 16, 256), BF16),
             vmem((16, 16, 256), BF16),
             dma, dma,
@@ -270,7 +277,7 @@
             dma, dma,
             dma((3,)), dma((2, 8, 4)),
             dma, dma,
-            dma, dma((3,)),
+            dma, dma((3, 2)),
             dma, dma,
             dma, dma,
             dma((5,)),

time: 69.4 us -> 68 us (0.980)
  Pallas kernels: 68.6 us -> 67.1 us
    pallas_call x1, Pallas kernels: 66.9 us -> 65.4 us  [body(): pl.pallas_call(kernel, out_shape=(jax.ShapeDtypeStruct((1, 128, 512), F32...]
where the time goes in v5:
time: 68 us; the launch traced here: 67.7 us
  Pallas kernels  67.1 us (99%)
    pallas_call x1, Pallas kernels, body(): pl.pallas_call(kernel, out_shape=(jax.ShapeDtypeStruct((1, 128, 512), F32...  65.4 us
    pallas_call x1, Pallas kernels, body(): pl.pallas_call(deliver, out_shape=tuple((jax.ShapeDtypeStruct(r.shape, F3...  1.68 us

profile of v5, /device:TPU:24, one launch (start us, length us, event | category | flops | bytes accessed | tf_op | source)
XLA Modules:
  0.0 67.7 jit_solution(931398177539174083)
XLA Ops:
  0.6 65.4 %takahashi.1 = (f32[1,128,512]{2,1,0:T(8,128)}, f32[1,8,512]{2,1,0:T(8,128)}) custom-call(bf16[1024,128]{1,0:T(8,128)(2,1)} %a_hbm.1, bf16[8,16,512]{2,1,0:T(8,128)(2,1)} %factor_hbm.1, bf16[8,512,512]{2,1,0:T(8,128)(2,1)} %inv_hbm.1, s32[8,32]{1,0:T(8,128)} %pattern_hbm.1), custom_call_target="tpu_custom_call" | custom-call | tf_op jit(solution)/shard_map/takahashi/pallas_call | solution.py:246
  66.1 1.7 %deliver.1 = (f32[1,128,512]{2,1,0:T(8,128)}, f32[1,8,512]{2,1,0:T(8,128)}) custom-call(f32[1,128,512]{2,1,0:T(8,128)} %get-tuple-element.4.panel_ref, f32[1,8,512]{2,1,0:T(8,128)} %get-tuple-element.5.diag_ref), custom_call_target="tpu_custom_call" | custom-call | tf_op jit(solution)/shard_map/deliver/pallas_call | solution.py:290

commit v6 on v5

--- a/solution.py
+++ b/solution.py
@@ -152,7 +152,7 @@
             part[yy, xx] = columns
             y_send[yy, xx] = columns.astype(BF16)
         if xx % 2 == 1:
-            for k in range(1, NY):
+            for k in (2, 1, 3):
                 ty, half = lax.rem(y + k, NY), pl.ds(xx - 1, 2)
                 send(
                     y_send.at[ty, half], y_recv.at[k, half], y_ss, y_rs.at[k - 1, xx // 2], device(x, ty, z, h)
@@ -160,7 +160,7 @@
     for half in range(2):
         pair = pl.ds(2 * half, 2)
         total = part[y, pair]
-        for k in range(1, NY):
+        for k in (1, 3, 2):
             all_in(y_recv.at[k, pair], y_rs.at[k - 1, half])
             total += y_recv[k, pair].astype(F32)
         o_send[pair] = total.astype(o_send.dtype)

time: 68 us -> 67.8 us (level)
  no operation moved by 1% of the time
where the time goes in v6:
time: 67.8 us; the launch traced here: 67.2 us
  Pallas kernels  66.6 us (98%)
    pallas_call x1, Pallas kernels, body(): pl.pallas_call(kernel, out_shape=(jax.ShapeDtypeStruct((1, 128, 512), F32...  64.9 us
    pallas_call x1, Pallas kernels, body(): pl.pallas_call(deliver, out_shape=tuple((jax.ShapeDtypeStruct(r.shape, F3...  1.68 us

profile of v6, /device:TPU:24, one launch (start us, length us, event | category | flops | bytes accessed | tf_op | source)
XLA Modules:
  0.0 67.2 jit_solution(15552497637267560075)
XLA Ops:
  0.6 64.9 %takahashi.1 = (f32[1,128,512]{2,1,0:T(8,128)}, f32[1,8,512]{2,1,0:T(8,128)}) custom-call(bf16[1024,128]{1,0:T(8,128)(2,1)} %a_hbm.1, bf16[8,16,512]{2,1,0:T(8,128)(2,1)} %factor_hbm.1, bf16[8,512,512]{2,1,0:T(8,128)(2,1)} %inv_hbm.1, s32[8,32]{1,0:T(8,128)} %pattern_hbm.1), custom_call_target="tpu_custom_call" | custom-call | tf_op jit(solution)/shard_map/takahashi/pallas_call | solution.py:246
  65.6 1.7 %deliver.1 = (f32[1,128,512]{2,1,0:T(8,128)}, f32[1,8,512]{2,1,0:T(8,128)}) custom-call(f32[1,128,512]{2,1,0:T(8,128)} %get-tuple-element.4.panel_ref, f32[1,8,512]{2,1,0:T(8,128)} %get-tuple-element.5.diag_ref), custom_call_target="tpu_custom_call" | custom-call | tf_op jit(solution)/shard_map/deliver/pallas_call | solution.py:290
